TPU v7x, 256 devices: a whole 4x4x8 slice. The times are simulated.
256 devices in a mesh: dp: 4 (over x), segment: 2 (over core), band: 32 (over z, y).
Axes of the slice: x: 4, y: 4, z: 8, core: 2. Of those that a mesh axis runs over, the one named last changes fastest.
Arguments:
- fields: bfloat16 [4, 2, 256, 16, 512], P('dp', None, 'band'), may hold values from -6 to 6
- cell_mask: int32 [4, 2, 256, 16], P('dp', None, 'band'), may hold values 0 or 1
- merge_weight: bfloat16 [2, 1024, 512], P('segment', 'dp'), may hold values from -0.1875 to 0.1875
- qkv_weight: bfloat16 [2, 512, 1536], P('segment', 'dp')
- out_weight: bfloat16 [2, 512, 512], P('segment', 'dp'), may hold values from -1 to 1
- norm_gain: bfloat16 [2, 512], P('segment', 'dp'), may hold values from 0.099609375 to 1.8984375
- out_cotangent: bfloat16 [4, 2, 256, 16, 512], P('dp', None, 'band'), may hold values from -6 to 6
Outputs:
- section_out: bfloat16 [2, 4, 2, 256, 16, 512], P('segment', 'dp', None, 'band')
- merge_grad: float32 [2, 1024, 512], P('segment', 'dp')
- qkv_grad: float32 [2, 512, 1536], P('segment', 'dp')
- out_grad: float32 [2, 512, 512], P('segment', 'dp')
- gain_grad: float32 [2, 512], P('segment', 'dp')
Inputs may be any that keep to these rules, and one draw needn't show every extreme that they name: `cell_mask`: 1 marks a cell whose keys may be attended.
All inputs are finite; a program needn't handle non-finite values. No bound on the sum of `cell_mask` on one device may be relied on, other than what follows from the above.
Results may differ from a plain program's by a relative error of at most 0.03.
Values may be sent and summed in bfloat16 or wider, within the bound.
A program may use at most 128 MiB of HBM per device.

v0:
```python
from functools import partial
import jax
import jax.numpy as jnp
from jax import lax
from jax.sharding import PartitionSpec as P

HEADS = 8
WH = 8
WW = 16
SH = 4
SW = 8
EPSILON = 1e-05
MASKED = -1e30


def padded(shard, sides, width):
    for axis, dim in sides:
        size, length = (lax.axis_size(axis), shard.shape[dim])
        up = [(i, (i + 1) % size) for i in range(size - 1)]
        down = [(j, i) for i, j in up]
        last = lax.slice_in_dim(shard, length - width, length, axis=dim)
        first = lax.slice_in_dim(shard, 0, width, axis=dim)
        before = lax.ppermute(last, axis, up)
        after = lax.ppermute(first, axis, down)
        shard = jnp.concatenate([before, shard, after], axis=dim)
    return shard


def partner(shard, axis, distance):
    return lax.ppermute(shard, axis, [(i, i ^ 1 << distance) for i in range(lax.axis_size(axis))])


def normalize(update):
    average = jnp.mean(update, axis=-1, keepdims=True)
    centered = update - average
    spread = jnp.mean(centered * centered, axis=-1, keepdims=True)
    inverse = lax.rsqrt(spread + EPSILON)
    return (centered * inverse, inverse)


def window_pattern(lon_count):
    query_index = jnp.arange(WH * lon_count, dtype=jnp.int32)
    key_index = jnp.arange(2 * WH * lon_count, dtype=jnp.int32)
    query_row = query_index // lon_count
    query_col = query_index % lon_count
    key_row = key_index // lon_count
    key_col = key_index % lon_count
    lat_same = ((query_row + SH) // WH)[:, None] == (key_row // WH)[None, :]
    lon_same = ((query_col + SW) // WW)[:, None] == ((key_col + SW) // WW)[None, :]
    self_key = ((query_row + SH)[:, None] == key_row[None, :]) & (
        query_col[:, None] == key_col[None, :]
    )
    return (lat_same & lon_same, self_key)


def attend(queries, keyvals, usable):
    row_count, lon_count, feature = queries.shape
    blocks = row_count // WH
    head_dim = feature // HEADS
    query_blocks = queries.reshape(blocks, WH * lon_count, HEADS, head_dim)
    kv_blocks = keyvals.reshape(blocks + 1, WH * lon_count, 2, HEADS, head_dim)
    key_pairs = jnp.concatenate([kv_blocks[:-1], kv_blocks[1:]], axis=1)
    use_blocks = usable.reshape(blocks + 1, WH * lon_count)
    use_pairs = jnp.concatenate([use_blocks[:-1], use_blocks[1:]], axis=1)
    inside, self_key = window_pattern(lon_count)
    allowed = inside[None] & (use_pairs[:, None, :] | self_key[None])
    scores = jnp.einsum(
        "nqhd,nkhd->nhqk", query_blocks, key_pairs[:, :, 0], preferred_element_type=jnp.float32
    ) * head_dim ** (-0.5)
    scores = jnp.where(allowed[:, None], scores, MASKED)
    highest = jnp.max(scores, axis=-1, keepdims=True)
    weights = jnp.exp(scores - highest)
    attn_prob = (weights / jnp.sum(weights, axis=-1, keepdims=True)).astype(jnp.bfloat16)
    mixture = jnp.einsum(
        "nhqk,nkhd->nqhd", attn_prob, key_pairs[:, :, 1], preferred_element_type=jnp.float32
    )
    return mixture.reshape(row_count, lon_count, feature).astype(jnp.bfloat16)


def guarded(active, function, operands):

    def skipped(values):
        return jax.tree.map(jnp.zeros_like, function(values))

    return lax.cond(active, function, skipped, operands)


def project(joined, merge_full, qkv_full, gain_full):
    update = jnp.einsum("rwj,jd->rwd", joined, merge_full, preferred_element_type=jnp.float32)
    normed, inverse = normalize(update)
    hidden = (normed * gain_full.astype(jnp.float32)).astype(jnp.bfloat16)
    projected = jnp.einsum("rwd,de->rwe", hidden, qkv_full, preferred_element_type=jnp.float32)
    feature = update.shape[-1]
    queries = projected[..., :feature].astype(jnp.bfloat16)
    keyvals = projected[..., feature:].astype(jnp.bfloat16)
    return (update, normed, inverse, hidden, queries, keyvals)


def section_forward(active, joined, usable, merge_full, qkv_full, gain_full, out_full):
    update, normed, inverse, hidden, queries, own_keys = guarded(
        active, lambda rows_own: project(rows_own, merge_full, qkv_full, gain_full), joined
    )
    keyvals = padded(own_keys, (("band", 0),), SH)

    def finish(operands):
        update_in, query_in, keyval_in, usable_in = operands
        mixture = attend(query_in, keyval_in, usable_in)
        result = (
            update_in
            + jnp.einsum("rwd,de->rwe", mixture, out_full, preferred_element_type=jnp.float32)
        ).astype(jnp.bfloat16)
        return (mixture, result)

    mixture, result = guarded(active, finish, (update, queries, keyvals, usable))
    return (result, (joined, normed, inverse, hidden, queries, keyvals, mixture))


def attend_back(out_full, operands):
    grad_out, queries, keyvals, mixture, usable = operands
    grad_mixture = jnp.einsum(
        "rwe,de->rwd", grad_out, out_full, preferred_element_type=jnp.float32
    ).astype(jnp.bfloat16)
    unused, pull_back = jax.vjp(
        lambda query_in, keyval_in: attend(query_in, keyval_in, usable), queries, keyvals
    )
    grad_query, grad_keyval = pull_back(grad_mixture)
    grad_outw = jnp.einsum("rwd,rwe->de", mixture, grad_out, preferred_element_type=jnp.float32)
    return (grad_query, grad_keyval, grad_outw)


def fold_rims(grad_keyval, row_count):
    rim_rows = jnp.concatenate([grad_keyval[:SH], grad_keyval[SH + row_count :]], axis=0)
    returned = padded(rim_rows, (("band", 0),), SH)
    own_part = grad_keyval[SH : SH + row_count].astype(jnp.float32)
    return jnp.concatenate(
        [
            own_part[:SH] + returned[:SH].astype(jnp.float32),
            own_part[SH : row_count - SH],
            own_part[row_count - SH :] + returned[3 * SH :].astype(jnp.float32),
        ],
        axis=0,
    ).astype(jnp.bfloat16)


def back_core(qkv_full, gain_full, grad_query, grad_keyown, grad_out, normed, inverse):
    grad_proj = jnp.concatenate([grad_query, grad_keyown], axis=-1)
    grad_hidden = jnp.einsum("rwe,de->rwd", grad_proj, qkv_full, preferred_element_type=jnp.float32)
    grad_normed = grad_hidden * gain_full.astype(jnp.float32)
    grad_update = (
        grad_out.astype(jnp.float32)
        + inverse
        * (
            grad_normed
            - jnp.mean(grad_normed, axis=-1, keepdims=True)
            - normed * jnp.mean(grad_normed * normed, axis=-1, keepdims=True)
        )
    ).astype(jnp.bfloat16)
    return (grad_proj, grad_hidden, grad_update)


def project_back(merge_part, qkv_full, gain_full, operands):
    grad_query, grad_keyown, grad_out, joined, normed, inverse, hidden = operands
    grad_proj, grad_hidden, grad_update = back_core(
        qkv_full, gain_full, grad_query, grad_keyown, grad_out, normed, inverse
    )
    grad_qkv = jnp.einsum("rwd,rwe->de", hidden, grad_proj, preferred_element_type=jnp.float32)
    grad_gain = jnp.sum(grad_hidden * normed, axis=(0, 1))
    grad_merge = jnp.einsum("rwj,rwd->jd", joined, grad_update, preferred_element_type=jnp.float32)
    grad_joined = jnp.einsum(
        "rwd,jd->rwj", grad_update, merge_part, preferred_element_type=jnp.float32
    )
    return (grad_joined, grad_merge, grad_qkv, grad_gain)


def store_slot(buffers, values, slot_index, active):

    def place_one(buffer, new_value):
        current = lax.dynamic_index_in_dim(buffer, slot_index, 0, keepdims=False)
        return lax.dynamic_update_index_in_dim(
            buffer, jnp.where(active, new_value, current), slot_index, 0
        )

    return jax.tree.map(place_one, buffers, values)


def body(fields, cell_mask, merge_weight, qkv_weight, out_weight, norm_gain, out_cotangent):
    merge_rows, qkv_rows, out_rows, gain_rows = (
        lax.all_gather(merge_weight, "dp", axis=1, tiled=True),
        lax.all_gather(qkv_weight, "dp", axis=1, tiled=True),
        lax.all_gather(out_weight, "dp", axis=1, tiled=True),
        lax.all_gather(norm_gain, "dp", axis=1, tiled=True),
    )
    merge_full = merge_rows[0]
    qkv_full = qkv_rows[0]
    out_full = out_rows[0]
    gain_full = gain_rows[0]
    inputs = fields[0]
    cotangent = out_cotangent[0]
    micro_count, row_count, lon_count, feature = inputs.shape
    mask_ext = padded(cell_mask[0], (("band", 1),), SH)
    usable_ext = mask_ext == 1
    section_count = lax.axis_size("segment")
    half_count = section_count // 2
    section_rank = lax.axis_index("segment")
    tick_count = half_count + micro_count - 1

    def to_partner(payload):
        payload = partner(payload, "segment", 0)
        return payload

    def forward_tick(phase, feed):

        def forward_one_tick(tick_index, state_in):
            sending, section_buf, stashed = state_in
            rank_local = section_rank - phase * half_count
            micro_index = tick_index - rank_local
            active = (
                (rank_local >= 0)
                & (rank_local < half_count)
                & (micro_index >= 0)
                & (micro_index < micro_count)
            )
            slot_index = jnp.clip(micro_index, 0, micro_count - 1)
            feed_now = lax.dynamic_index_in_dim(feed, slot_index, 0, keepdims=False)
            joined = jnp.concatenate([feed_now, feed_now], axis=-1)
            usable = lax.dynamic_index_in_dim(usable_ext, slot_index, 0, keepdims=False)
            result, record = section_forward(
                active, joined, usable, merge_full, qkv_full, gain_full, out_full
            )
            section_buf = store_slot(section_buf, result, slot_index, active)
            stashed = store_slot(stashed, record, slot_index, active)
            return (result, section_buf, stashed)

        return forward_one_tick

    def backward_tick(phase, feed, stashed):
        merge_part = merge_full if phase == 0 else merge_full[:feature]

        def backward_one_tick(tick_index, state_in):
            sending, skip_buf, grad_sums = state_in
            rank_local = section_count - 1 - section_rank - phase * half_count
            micro_index = tick_index - rank_local
            active = (
                (rank_local >= 0)
                & (rank_local < half_count)
                & (micro_index >= 0)
                & (micro_index < micro_count)
            )
            slot_index = jnp.clip(micro_index, 0, micro_count - 1)
            grad_out = lax.dynamic_index_in_dim(feed, slot_index, 0, keepdims=False)
            joined, normed, inverse, hidden, queries, keyvals, mixture = jax.tree.map(
                lambda buffer: lax.dynamic_index_in_dim(buffer, slot_index, 0, keepdims=False),
                stashed,
            )
            usable = lax.dynamic_index_in_dim(usable_ext, slot_index, 0, keepdims=False)
            grad_query, grad_keyval, grad_outw = guarded(
                active,
                partial(attend_back, out_full),
                (grad_out, queries, keyvals, mixture, usable),
            )
            grad_keyown = fold_rims(grad_keyval, row_count)
            grad_joined, grad_merge, grad_qkv, grad_gain = guarded(
                active,
                partial(project_back, merge_part, qkv_full, gain_full),
                (grad_query, grad_keyown, grad_out, joined, normed, inverse, hidden),
            )
            grad_sums = (
                grad_sums[0] + grad_merge,
                grad_sums[1] + grad_qkv,
                grad_sums[2] + grad_outw,
                grad_sums[3] + grad_gain,
            )
            grad_chain = grad_joined[..., :feature].astype(jnp.bfloat16)
            if phase == 0:
                grad_side = grad_joined[..., feature:].astype(jnp.bfloat16)
                toward = jnp.where(
                    section_rank == half_count,
                    (grad_chain.astype(jnp.float32) + grad_side.astype(jnp.float32)).astype(
                        jnp.bfloat16
                    ),
                    grad_side,
                )
                skip_buf = store_slot(skip_buf, toward, slot_index, active)
            return (grad_chain, skip_buf, grad_sums)

        return backward_one_tick

    stashed = (
        jnp.zeros((micro_count, row_count, lon_count, 2 * feature), jnp.bfloat16),
        jnp.zeros((micro_count, row_count, lon_count, feature), jnp.float32),
        jnp.zeros((micro_count, row_count, lon_count, 1), jnp.float32),
        jnp.zeros((micro_count, row_count, lon_count, feature), jnp.bfloat16),
        jnp.zeros((micro_count, row_count, lon_count, feature), jnp.bfloat16),
        jnp.zeros((micro_count, row_count + 2 * SH, lon_count, 2 * feature), jnp.bfloat16),
        jnp.zeros((micro_count, row_count, lon_count, feature), jnp.bfloat16),
    )
    section_buf = jnp.zeros((micro_count, row_count, lon_count, feature), jnp.bfloat16)
    spare_rows = jnp.zeros((row_count, lon_count, feature), jnp.bfloat16)
    unused, section_buf, stashed = lax.fori_loop(
        0, tick_count, forward_tick(0, inputs), (spare_rows, section_buf, stashed)
    )
    skip_in = to_partner(section_buf)
    unused, section_buf, stashed = lax.fori_loop(
        0, tick_count, forward_tick(1, skip_in), (spare_rows, section_buf, stashed)
    )
    grad_sums = (
        jnp.zeros((2 * feature, feature), jnp.float32),
        jnp.zeros((feature, 3 * feature), jnp.float32),
        jnp.zeros((feature, feature), jnp.float32),
        jnp.zeros((feature,), jnp.float32),
    )
    unused, skip_buf, grad_sums = lax.fori_loop(
        0,
        tick_count,
        backward_tick(0, cotangent, stashed),
        (spare_rows, jnp.zeros_like(section_buf), grad_sums),
    )
    skip_back = to_partner(skip_buf)
    unused, skip_buf, grad_sums = lax.fori_loop(
        0, tick_count, backward_tick(1, skip_back, stashed), (spare_rows, skip_buf, grad_sums)
    )
    section_home = section_buf[None, None]
    merge_part_sum, qkv_part_sum, out_part_sum, gain_part_sum = (
        lax.psum_scatter(
            grad_sums[0][None].astype(jnp.bfloat16), "dp", scatter_dimension=1, tiled=True
        ).astype(jnp.float32),
        lax.psum_scatter(
            grad_sums[1][None].astype(jnp.bfloat16), "dp", scatter_dimension=1, tiled=True
        ).astype(jnp.float32),
        lax.psum_scatter(
            grad_sums[2][None].astype(jnp.bfloat16), "dp", scatter_dimension=1, tiled=True
        ).astype(jnp.float32),
        lax.psum_scatter(
            grad_sums[3][None].astype(jnp.bfloat16), "dp", scatter_dimension=1, tiled=True
        ).astype(jnp.float32),
    )
    merge_grad, qkv_grad, out_grad, gain_grad = (
        lax.psum(merge_part_sum.astype(jnp.bfloat16), "band").astype(jnp.float32),
        lax.psum(qkv_part_sum.astype(jnp.bfloat16), "band").astype(jnp.float32),
        lax.psum(out_part_sum.astype(jnp.bfloat16), "band").astype(jnp.float32),
        lax.psum(gain_part_sum.astype(jnp.bfloat16), "band").astype(jnp.float32),
    )
    return (section_home, merge_grad, qkv_grad, out_grad, gain_grad)


def solution(mesh):
    return jax.shard_map(
        body,
        mesh=mesh,
        in_specs=(
            P("dp", None, "band", None, None),
            P("dp", None, "band", None),
            P("segment", "dp", None),
            P("segment", "dp", None),
            P("segment", "dp", None),
            P("segment", "dp"),
            P("dp", None, "band", None, None),
        ),
        out_specs=(
            P("segment", "dp", None, "band", None, None),
            P("segment", "dp", None),
            P("segment", "dp", None),
            P("segment", "dp", None),
            P("segment", "dp"),
        ),
        check_vma=False,
    )
```

profile of v0, /device:TPU:2, one launch (start us, length us, event | category | flops | bytes accessed | tf_op | source)
XLA Modules:
  0.0 875.8 jit_solution(191999634789803929)
XLA Ops:
  9.5 3.5 collective-permute-start.8
  14.3 13.6 %all_gather.15 = bf16[1,512,512]{2,1,0:T(8,128)(2,1)S(1)} all-gather(bf16[1,128,512]{2,1,0:T(8,128)(2,1)} %param.35), channel_id=1, replica_groups=mesh['dp'=4,'segment'=2,'band'=32] {'dp'}, dimensions={1}, use_global_device_ids=true | all-gather | bytes 655360 | tf_op jit(solution)/shard_map/all_gather | solution.py:190
  27.9 7.6 all_gather.13
  38.2 32.2 %all-gather.5.cloned.1.call-done = bf16[1,512,1536]{2,1,0:T(8,128)(2,1)} async-done(((bf16[1,128,1536]{2,1,0:T(8,128)(2,1)}), bf16[1,512,1536]{2,1,0:T(8,128)(2,1)}) %all-gather.5.cloned.1.call-update) | async-done | bytes 1572880 | tf_op jit(solution)/shard_map/all_gather | solution.py:189
  76.2 116.6 %while.103 = (s32[]{:T(128)}, bf16[2,8,16,512]{3,2,1,0:T(8,128)(2,1)}, bf16[2,8,16,1024]{3,2,1,0:T(8,128)(2,1)}, f32[2,8,16,512]{3,2,1,0:T(8,128)}, f32[2,8,16,1...) while((s32[]{:T(128)}, ...), condition=%wide.region_9.10_spmd, body=%wide.region_0.9_spmd.sunk | while | flops 477448448 | bytes 26721116 | solution.py:299
  77.2 5.2 conditional.18
  84.5 5.2 collective-permute-start.1
  103.1 27.5 %conditional.19 = (bf16[8,16,512]{2,1,0:T(8,128)(2,1)}, bf16[8,16,512]{2,1,0:T(8,128)(2,1)}) conditional(s32[]{:T(128)} %convert_element_type.561, () %tuple.323, (bf16[16,16,1024]{2,1,0:T(8,128)(2,1)}, pred[2,16,16]{2,1,0:T(8,128)(4,1)S(1)}, s32[]{:T(128)}, bf16[8,16,512]{2,1,0:T(8,128)(2,1)S(1)}, bf16[512,512]{1,0:T(8,128)(2,1)S(1)}, ...), branch_computations={%region_5.5_spmd, %region_6.8_spmd} | conditional | flops 137315840 | bytes 8476452 | solution.py:85
  121.1 3.2 fusion.210
  135.4 5.2 conditional.18
  142.7 5.2 collective-permute-start.1
  161.4 27.5 %conditional.19 = (bf16[8,16,512]{2,1,0:T(8,128)(2,1)}, bf16[8,16,512]{2,1,0:T(8,128)(2,1)}) conditional(s32[]{:T(128)} %convert_element_type.561, () %tuple.323, (bf16[16,16,1024]{2,1,0:T(8,128)(2,1)}, pred[2,16,16]{2,1,0:T(8,128)(4,1)S(1)}, s32[]{:T(128)}, bf16[8,16,512]{2,1,0:T(8,128)(2,1)S(1)}, bf16[512,512]{1,0:T(8,128)(2,1)S(1)}, ...), branch_computations={%region_5.5_spmd, %region_6.8_spmd} | conditional | flops 137315840 | bytes 8476452 | solution.py:85
  179.4 3.2 fusion.210
  194.7 54.8 %while.104 = (s32[]{:T(128)}, bf16[2,8,16,512]{3,2,1,0:T(8,128)(2,1)}, bf16[2,8,16,1024]{3,2,1,0:T(8,128)(2,1)}, f32[2,8,16,512]{3,2,1,0:T(8,128)}, f32[2,8,16,1...) while((s32[]{:T(128)}, ...), condition=%wide.region_19.20_spmd, body=%wide.region_10.19_spmd.sunk | while | flops 477448448 | bytes 26721116 | solution.py:303
  199.2 5.2 collective-permute-start.3
  226.6 5.2 collective-permute-start.3
  250.3 60.6 %while.106 = (s32[]{:T(128)}, bf16[2,8,16,512]{3,2,1,0:T(8,128)(2,1)}, f32[1024,512]{1,0:T(8,128)}, f32[512,1536]{1,0:T(8,128)}, f32[512,512]{1,0:T(8,128)}, /*i...) while((s32[]{:T(128)}, ...), condition=%wide.region_33.34_spmd.clone, body=%wide.region_20.33_spmd.clone.sunk | while | flops 992495872 | bytes 121524072 | solution.py:312
  255.1 4.3 collective-permute-start.6
  272.8 3.7 select_add_fusion.8
  284.2 6.7 collective-permute-start.6
  292.2 2.7 select_add_fusion.10
  303.3 4.3 select_add_fusion.8
  310.9 143.5 %collective-permute-start.11 = (bf16[2,8,16,512]{3,2,1,0:T(8,128)(2,1)}, bf16[2,8,16,512]{3,2,1,0:T(8,128)(2,1)S(1)}, u32[]{:S(2)}, u32[]{:S(2)}) collective-permute-start(bf16[2,8,16,512]{3,2,1,0:T(8,128)(2,1)} %get-tuple-element.2101), channel_id=1, source_target_pairs={{0,32},{32,0},{1,33},{33,1},{2,34},{34,2},{3,35},{35,3},{4,36},{36... | collective-permute-start | bytes 786440 | tf_op jit(solution)/shard_map/ppermute | solution.py:30
  455.8 131.6 %while.105 = (s32[]{:T(128)}, f32[1024,512]{1,0:T(8,128)}, f32[512,1536]{1,0:T(8,128)}, f32[512,512]{1,0:T(8,128)}, f32[512]{0:T(512)}, /*index=5*/s32[]{:T(128)...) while((s32[]{:T(128)}, f32[1024,512]{1,0:T(8,128)}, ...), condition=%wide.region_47.48_spmd, body=%wide.region_34.47_spmd.sunk | while | flops 856311552 | bytes 123788608 | solution.py:319
  456.6 35.0 %conditional.22 = (bf16[8,16,512]{2,1,0:T(8,128)(2,1)}, bf16[16,16,1024]{2,1,0:T(8,128)(2,1)}, f32[512,512]{1,0:T(8,128)}) conditional(s32[]{:T(128)} %convert_element_type.565, () %tuple.339, (pred[2,16,16]{2,1,0:T(8,128)(4,1)S(1)}, s32[]{:T(128)}, bf16[8,16,512]{2,1,0:T(8,128)(2,1)}, bf16[512,512]{1,0:T(8,128)(2,1)S(1)}, ...), branch_computations={%region_35.35_spmd, %region_36.41_spmd} | conditional | flops 316294400 | bytes 26212748 | solution.py:85
  486.3 2.7 copy.87
  489.0 2.6 reshape.1705
  492.6 6.2 collective-permute-start.4
  502.9 2.8 collective-permute-done.5
  506.9 6.1 conditional.23
  509.6 2.8 convolution_bitcast_fusion.3
  514.7 4.3 add.947
  522.9 35.0 %conditional.22 = (bf16[8,16,512]{2,1,0:T(8,128)(2,1)}, bf16[16,16,1024]{2,1,0:T(8,128)(2,1)}, f32[512,512]{1,0:T(8,128)}) conditional(s32[]{:T(128)} %convert_element_type.565, () %tuple.339, (pred[2,16,16]{2,1,0:T(8,128)(4,1)S(1)}, s32[]{:T(128)}, bf16[8,16,512]{2,1,0:T(8,128)(2,1)}, bf16[512,512]{1,0:T(8,128)(2,1)S(1)}, ...), branch_computations={%region_35.35_spmd, %region_36.41_spmd} | conditional | flops 316294400 | bytes 26212748 | solution.py:85
  552.6 2.7 copy.87
  555.3 2.6 reshape.1705
  558.9 4.0 collective-permute-start.4
  567.1 4.0 collective-permute-done.5
  572.2 6.1 conditional.23
  574.9 2.8 convolution_bitcast_fusion.3
  580.0 4.3 add.947
  589.6 2.7 convert_bitcast_fusion.1
  592.4 3.2 convert_bitcast_fusion
  596.6 27.5 %reduce-scatter.11.cloned.1.call-done = bf16[1,128,512]{2,1,0:T(8,128)(2,1)} async-done(((bf16[1,512,512]{2,1,0:T(8,128)(2,1)}), bf16[1,128,512]{2,1,0:T(8,128)(2,1)}) %reduce-scatter.11.cloned.1.call-update) | async-done | bytes 131088 | tf_op jit(solution)/shard_map/reduce_scatter | solution.py:330
  624.1 28.4 %reduce-scatter.7.cloned.1.call-done = bf16[1,256,512]{2,1,0:T(8,128)(2,1)} async-done(((bf16[1,1024,512]{2,1,0:T(8,128)(2,1)}), bf16[1,256,512]{2,1,0:T(8,128)(2,1)}) %reduce-scatter.7.cloned.1.call-update) | async-done | bytes 262160 | tf_op jit(solution)/shard_map/reduce_scatter | solution.py:324
  652.5 31.1 %reduce-scatter.9.cloned.1.call-done = bf16[1,128,1536]{2,1,0:T(8,128)(2,1)} async-done(((bf16[1,512,1536]{2,1,0:T(8,128)(2,1)}), bf16[1,128,1536]{2,1,0:T(8,128)(2,1)}) %reduce-scatter.9.cloned.1.call-update) | async-done | bytes 393232 | tf_op jit(solution)/shard_map/reduce_scatter | solution.py:327
  683.6 25.3 %reduce-scatter.13.cloned.1.call-done = bf16[128,1]{1,0:T(8,128)(2,1)} async-done(((bf16[512,1]{1,0:T(8,128)(2,1)}), bf16[128,1]{1,0:T(8,128)(2,1)}) %reduce-scatter.13.cloned.1.call-update) | async-done | bytes 272
  709.8 75.3 %psum.31 = bf16[1,128]{1,0:T(2,128)(2,1)S(1)} all-reduce(bf16[1,128]{1,0:T(2,128)(2,1)S(1)} %copy.91), channel_id=1, replica_groups=mesh['dp'=4,'segment'=2,'band'=32] {'band'}, use_global_device_ids=true, to_apply=%region_55.56 | all-reduce | flops 128 | bytes 512 | tf_op jit(solution)/shard_map/psum | solution.py:341
  785.6 77.6 %all-reduce.11.cloned.1.call-done = (bf16[1,256,512]{2,1,0:T(8,128)(2,1)}, bf16[1,128,1536]{2,1,0:T(8,128)(2,1)}, bf16[1,128,512]{2,1,0:T(8,128)(2,1)}) async-done(((bf16[1,256,512]{2,1,0:T(8,128)(2,1)}, bf16[1,128,1536]{2,1,0:T(8,128)(2,1)}, bf16[1,128,512]{2,1,0:T(8,128)(2,1)}), (bf16[1,256,512]{2,1,0:T(8,128)(2,1)}, bf16[1,128,1536]{2,1,0:T(8,128)(2,1)}, ...) | async-done | bytes 786448 | tf_op jit(solution)/shard_map/psum | solution.py:338
  (482 shorter events, 310.5 us)
Async XLA Ops:
  7.2 31.1 %all-gather.3.cloned.1.call-start = ((), (), s32[]{:S(2)}) async-start(), calls=%async_computation.4 | async-start | bytes 1310720 | tf_op jit(solution)/shard_map/all_gather | solution.py:188
  7.9 62.5 %all-gather.5.cloned.1.call-start = ((), (), s32[]{:S(2)}) async-start(), calls=%async_computation.5 | async-start | bytes 1966080 | tf_op jit(solution)/shard_map/all_gather | solution.py:189
  8.6 615.4 %reduce-scatter.11.cloned.1.call-start = ((), (), s32[]{:S(2)}) async-start(), calls=%async_computation.8 | async-start | bytes 655360 | tf_op jit(solution)/shard_map/reduce_scatter | solution.py:330
  9.5 26.0 %collective-permute-start.8 = (s32[2,4,16]{2,1,0:T(4,128)S(1)}, s32[2,4,16]{2,1,0:T(4,128)S(1)}, u32[]{:S(2)}, u32[]{:S(2)}) collective-permute-start(s32[2,4,16]{2,1,0:T(4,128)S(1)} %get-tuple-element.2527), channel_id=1, source_target_pairs={{0,1},{1,2},{2,3},{3,4},{4,5},{5,6},{6,7},{7,8},{8,9},{9,10},{10,1... | collective-permute-start | bytes 1544 | tf_op jit(solution)/shard_map/ppermute | solution.py:23
  12.9 22.5 %collective-permute-start.9 = (s32[2,4,16]{2,1,0:T(4,128)S(1)}, s32[2,4,16]{2,1,0:T(4,128)S(1)}, u32[]{:S(2)}, u32[]{:S(2)}) collective-permute-start(s32[2,4,16]{2,1,0:T(4,128)S(1)} %get-tuple-element.2528), channel_id=1, source_target_pairs={{1,0},{2,1},{3,2},{4,3},{5,4},{6,5},{7,6},{8,7},{9,8},{10,9},{11,1... | collective-permute-start | bytes 1544 | tf_op jit(solution)/shard_map/ppermute | solution.py:24
  38.2 38.0 %copy-start.9 = (bf16[1,1024,512]{2,1,0:T(8,128)(2,1)S(1)}, bf16[1,1024,512]{2,1,0:T(8,128)(2,1)}, u32[]{:S(2)}) copy-start(bf16[1,1024,512]{2,1,0:T(8,128)(2,1)} %all-gather.3.cloned.1.call-done) | copy-start | bytes 3145732
  70.4 5.8 copy-start
  82.4 14.0 %copy-start.25 = (bf16[2,8,16,512]{3,2,1,0:T(8,128)(2,1)S(1)}, bf16[2,8,16,512]{3,2,1,0:T(8,128)(2,1)}, u32[]{:S(2)}) copy-start(bf16[2,8,16,512]{3,2,1,0:T(8,128)(2,1)} %get-tuple-element.3164) | copy-start | bytes 786436 | tf_op jit(solution)/shard_map/while
  82.4 16.3 %copy-start.31 = (bf16[2,8,16,512]{3,2,1,0:T(8,128)(2,1)S(1)}, bf16[2,8,16,512]{3,2,1,0:T(8,128)(2,1)}, u32[]{:S(2)}) copy-start(bf16[2,8,16,512]{3,2,1,0:T(8,128)(2,1)} %get-tuple-element.3160) | copy-start | bytes 786436 | tf_op jit(solution)/shard_map/while
  83.2 18.0 %collective-permute-start = (bf16[4,16,1024]{2,1,0:T(8,128)(2,1)}, bf16[4,16,1024]{2,1,0:T(8,128)(2,1)}, u32[]{:S(2)}, u32[]{:S(2)}) collective-permute-start(bf16[4,16,1024]{2,1,0:T(8,128)(2,1)} %get-tuple-element.2975), channel_id=1, source_target_pairs={{1,0},{2,1},{3,2},{4,3},{5,4},{6,5},{7,6},{8,7},{9,8},{10,9},{11,1... | collective-permute-start | bytes 393224 | tf_op jit(solution)/shard_map/while/body/eval_jaxpr/ppermute | solution.py:24
  84.5 16.8 %collective-permute-start.1 = (bf16[4,16,1024]{2,1,0:T(8,128)(2,1)}, bf16[4,16,1024]{2,1,0:T(8,128)(2,1)}, u32[]{:S(2)}, u32[]{:S(2)}) collective-permute-start(bf16[4,16,1024]{2,1,0:T(8,128)(2,1)} %get-tuple-element.2976), channel_id=1, source_target_pairs={{0,1},{1,2},{2,3},{3,4},{4,5},{5,6},{6,7},{7,8},{8,9},{9,10},{10,1... | collective-permute-start | bytes 393224 | tf_op jit(solution)/shard_map/while/body/eval_jaxpr/ppermute | solution.py:23
  140.7 14.0 %copy-start.25 = (bf16[2,8,16,512]{3,2,1,0:T(8,128)(2,1)S(1)}, bf16[2,8,16,512]{3,2,1,0:T(8,128)(2,1)}, u32[]{:S(2)}) copy-start(bf16[2,8,16,512]{3,2,1,0:T(8,128)(2,1)} %get-tuple-element.3164) | copy-start | bytes 786436 | tf_op jit(solution)/shard_map/while
  140.7 16.3 %copy-start.31 = (bf16[2,8,16,512]{3,2,1,0:T(8,128)(2,1)S(1)}, bf16[2,8,16,512]{3,2,1,0:T(8,128)(2,1)}, u32[]{:S(2)}) copy-start(bf16[2,8,16,512]{3,2,1,0:T(8,128)(2,1)} %get-tuple-element.3160) | copy-start | bytes 786436 | tf_op jit(solution)/shard_map/while
  141.5 18.0 %collective-permute-start = (bf16[4,16,1024]{2,1,0:T(8,128)(2,1)}, bf16[4,16,1024]{2,1,0:T(8,128)(2,1)}, u32[]{:S(2)}, u32[]{:S(2)}) collective-permute-start(bf16[4,16,1024]{2,1,0:T(8,128)(2,1)} %get-tuple-element.2975), channel_id=1, source_target_pairs={{1,0},{2,1},{3,2},{4,3},{5,4},{6,5},{7,6},{8,7},{9,8},{10,9},{11,1... | collective-permute-start | bytes 393224 | tf_op jit(solution)/shard_map/while/body/eval_jaxpr/ppermute | solution.py:24
  142.7 16.8 %collective-permute-start.1 = (bf16[4,16,1024]{2,1,0:T(8,128)(2,1)}, bf16[4,16,1024]{2,1,0:T(8,128)(2,1)}, u32[]{:S(2)}, u32[]{:S(2)}) collective-permute-start(bf16[4,16,1024]{2,1,0:T(8,128)(2,1)} %get-tuple-element.2976), channel_id=1, source_target_pairs={{0,1},{1,2},{2,3},{3,4},{4,5},{5,6},{6,7},{7,8},{8,9},{9,10},{10,1... | collective-permute-start | bytes 393224 | tf_op jit(solution)/shard_map/while/body/eval_jaxpr/ppermute | solution.py:23
  192.8 1.9 collective-permute-start.10
  197.1 14.0 %copy-start.27 = (bf16[2,8,16,512]{3,2,1,0:T(8,128)(2,1)S(1)}, bf16[2,8,16,512]{3,2,1,0:T(8,128)(2,1)}, u32[]{:S(2)}) copy-start(bf16[2,8,16,512]{3,2,1,0:T(8,128)(2,1)} %get-tuple-element.3224) | copy-start | bytes 786436 | tf_op jit(solution)/shard_map/while
  197.2 15.4 %copy-start.32 = (bf16[2,8,16,512]{3,2,1,0:T(8,128)(2,1)S(1)}, bf16[2,8,16,512]{3,2,1,0:T(8,128)(2,1)}, u32[]{:S(2)}) copy-start(bf16[2,8,16,512]{3,2,1,0:T(8,128)(2,1)} %get-tuple-element.3220) | copy-start | bytes 786436 | tf_op jit(solution)/shard_map/while
  197.9 17.1 %collective-permute-start.2 = (bf16[4,16,1024]{2,1,0:T(8,128)(2,1)}, bf16[4,16,1024]{2,1,0:T(8,128)(2,1)}, u32[]{:S(2)}, u32[]{:S(2)}) collective-permute-start(bf16[4,16,1024]{2,1,0:T(8,128)(2,1)} %get-tuple-element.3006), channel_id=1, source_target_pairs={{1,0},{2,1},{3,2},{4,3},{5,4},{6,5},{7,6},{8,7},{9,8},{10,9},{11,1... | collective-permute-start | bytes 393224 | tf_op jit(solution)/shard_map/while/body/eval_jaxpr/ppermute | solution.py:24
  199.2 15.8 %collective-permute-start.3 = (bf16[4,16,1024]{2,1,0:T(8,128)(2,1)}, bf16[4,16,1024]{2,1,0:T(8,128)(2,1)}, u32[]{:S(2)}, u32[]{:S(2)}) collective-permute-start(bf16[4,16,1024]{2,1,0:T(8,128)(2,1)} %get-tuple-element.3007), channel_id=1, source_target_pairs={{0,1},{1,2},{2,3},{3,4},{4,5},{5,6},{6,7},{7,8},{8,9},{9,10},{10,1... | collective-permute-start | bytes 393224 | tf_op jit(solution)/shard_map/while/body/eval_jaxpr/ppermute | solution.py:23
  224.6 14.0 %copy-start.27 = (bf16[2,8,16,512]{3,2,1,0:T(8,128)(2,1)S(1)}, bf16[2,8,16,512]{3,2,1,0:T(8,128)(2,1)}, u32[]{:S(2)}) copy-start(bf16[2,8,16,512]{3,2,1,0:T(8,128)(2,1)} %get-tuple-element.3224) | copy-start | bytes 786436 | tf_op jit(solution)/shard_map/while
  224.6 15.4 %copy-start.32 = (bf16[2,8,16,512]{3,2,1,0:T(8,128)(2,1)S(1)}, bf16[2,8,16,512]{3,2,1,0:T(8,128)(2,1)}, u32[]{:S(2)}) copy-start(bf16[2,8,16,512]{3,2,1,0:T(8,128)(2,1)} %get-tuple-element.3220) | copy-start | bytes 786436 | tf_op jit(solution)/shard_map/while
  225.3 17.1 %collective-permute-start.2 = (bf16[4,16,1024]{2,1,0:T(8,128)(2,1)}, bf16[4,16,1024]{2,1,0:T(8,128)(2,1)}, u32[]{:S(2)}, u32[]{:S(2)}) collective-permute-start(bf16[4,16,1024]{2,1,0:T(8,128)(2,1)} %get-tuple-element.3006), channel_id=1, source_target_pairs={{1,0},{2,1},{3,2},{4,3},{5,4},{6,5},{7,6},{8,7},{9,8},{10,9},{11,1... | collective-permute-start | bytes 393224 | tf_op jit(solution)/shard_map/while/body/eval_jaxpr/ppermute | solution.py:24
  226.6 15.8 %collective-permute-start.3 = (bf16[4,16,1024]{2,1,0:T(8,128)(2,1)}, bf16[4,16,1024]{2,1,0:T(8,128)(2,1)}, u32[]{:S(2)}, u32[]{:S(2)}) collective-permute-start(bf16[4,16,1024]{2,1,0:T(8,128)(2,1)} %get-tuple-element.3007), channel_id=1, source_target_pairs={{0,1},{1,2},{2,3},{3,4},{4,5},{5,6},{6,7},{7,8},{8,9},{9,10},{10,1... | collective-permute-start | bytes 393224 | tf_op jit(solution)/shard_map/while/body/eval_jaxpr/ppermute | solution.py:23
  253.4 11.6 %copy-start.21 = (bf16[8,16,512]{2,1,0:T(8,128)(2,1)}, bf16[8,16,512]{2,1,0:T(8,128)(2,1)S(1)}, u32[]{:S(2)}) copy-start(bf16[8,16,512]{2,1,0:T(8,128)(2,1)S(1)} %get-tuple-element.3070) | copy-start | bytes 393220 | tf_op jit(solution)/shard_map/while
  255.1 11.4 %collective-permute-start.6 = (bf16[4,16,1024]{2,1,0:T(8,128)(2,1)}, bf16[4,16,1024]{2,1,0:T(8,128)(2,1)}, u32[]{:S(2)}, u32[]{:S(2)}) collective-permute-start(bf16[4,16,1024]{2,1,0:T(8,128)(2,1)} %get-tuple-element.3072), channel_id=1, source_target_pairs={{0,1},{1,2},{2,3},{3,4},{4,5},{5,6},{6,7},{7,8},{8,9},{9,10},{10,1... | collective-permute-start | bytes 393224 | tf_op jit(solution)/shard_map/while/body/eval_jaxpr/ppermute | solution.py:23
  259.4 8.4 collective-permute-start.7
  282.5 14.2 %copy-start.21 = (bf16[8,16,512]{2,1,0:T(8,128)(2,1)}, bf16[8,16,512]{2,1,0:T(8,128)(2,1)S(1)}, u32[]{:S(2)}) copy-start(bf16[8,16,512]{2,1,0:T(8,128)(2,1)S(1)} %get-tuple-element.3070) | copy-start | bytes 393220 | tf_op jit(solution)/shard_map/while
  284.2 14.1 %collective-permute-start.6 = (bf16[4,16,1024]{2,1,0:T(8,128)(2,1)}, bf16[4,16,1024]{2,1,0:T(8,128)(2,1)}, u32[]{:S(2)}, u32[]{:S(2)}) collective-permute-start(bf16[4,16,1024]{2,1,0:T(8,128)(2,1)} %get-tuple-element.3072), channel_id=1, source_target_pairs={{0,1},{1,2},{2,3},{3,4},{4,5},{5,6},{6,7},{7,8},{8,9},{9,10},{10,1... | collective-permute-start | bytes 393224 | tf_op jit(solution)/shard_map/while/body/eval_jaxpr/ppermute | solution.py:23
  290.9 7.4 collective-permute-start.7
  310.9 144.9 %collective-permute-start.11 = (bf16[2,8,16,512]{3,2,1,0:T(8,128)(2,1)}, bf16[2,8,16,512]{3,2,1,0:T(8,128)(2,1)S(1)}, u32[]{:S(2)}, u32[]{:S(2)}) collective-permute-start(bf16[2,8,16,512]{3,2,1,0:T(8,128)(2,1)} %get-tuple-element.2101), channel_id=1, source_target_pairs={{0,32},{32,0},{1,33},{33,1},{2,34},{34,2},{3,35},{35,3},{4,36},{36... | collective-permute-start | bytes 786440 | tf_op jit(solution)/shard_map/ppermute | solution.py:30
  456.6 43.5 %copy-start.10 = (f32[512,512]{1,0:T(8,128)S(1)}, f32[512,512]{1,0:T(8,128)}, u32[]{:S(2)}) copy-start(f32[512,512]{1,0:T(8,128)} %get-tuple-element.3359) | copy-start | bytes 3145732 | tf_op jit(solution)/shard_map/while
  492.6 10.3 %collective-permute-start.4 = (bf16[4,16,1024]{2,1,0:T(8,128)(2,1)S(1)}, bf16[4,16,1024]{2,1,0:T(8,128)(2,1)}, u32[]{:S(2)}, u32[]{:S(2)}) collective-permute-start(bf16[4,16,1024]{2,1,0:T(8,128)(2,1)S(1)} %get-tuple-element.3040), channel_id=1, source_target_pairs={{0,1},{1,2},{2,3},{3,4},{4,5},{5,6},{6,7},{7,8},{8,9},{9,10},{10,1... | collective-permute-start | bytes 393224 | tf_op jit(solution)/shard_map/while/body/eval_jaxpr/ppermute | solution.py:23
  498.8 7.0 collective-permute-start.5
  500.1 6.7 copy-start.17
  500.1 6.7 copy-start.22
  500.1 6.7 copy-start.30
  522.9 41.3 %copy-start.10 = (f32[512,512]{1,0:T(8,128)S(1)}, f32[512,512]{1,0:T(8,128)}, u32[]{:S(2)}) copy-start(f32[512,512]{1,0:T(8,128)} %get-tuple-element.3359) | copy-start | bytes 3145732 | tf_op jit(solution)/shard_map/while
  558.9 8.2 collective-permute-start.4
  562.9 8.1 collective-permute-start.5
  564.2 7.9 copy-start.17
  564.3 7.9 copy-start.22
  564.3 7.9 copy-start.30
  565.9 6.3 copy-start.11
  589.5 62.9 %reduce-scatter.7.cloned.1.call-start = ((), (), s32[]{:S(2)}) async-start(), calls=%async_computation.6 | async-start | bytes 1310720 | tf_op jit(solution)/shard_map/reduce_scatter | solution.py:324
  592.4 91.3 %reduce-scatter.9.cloned.1.call-start = ((), (), s32[]{:S(2)}) async-start(), calls=%async_computation.7 | async-start | bytes 1966080 | tf_op jit(solution)/shard_map/reduce_scatter | solution.py:327
  595.7 113.3 %reduce-scatter.13.cloned.1.call-start = ((), (), s32[]{:S(2)}) async-start(), calls=%async_computation.9 | async-start | bytes 163840
  596.5 266.7 %all-reduce.11.cloned.1.call-start = ((), (), s32[]{:S(2)}) async-start(), calls=%async_computation.10 | async-start | bytes 1572864 | tf_op jit(solution)/shard_map/psum | solution.py:338
  (48 other events, 108.4 us)
Sparse Core Ops, SparseCore 0:
  9.8 28.3 all-gather.2
  40.0 30.3 all-gather.4
  589.7 34.3 reduce-scatter.10
  626.5 25.9 reduce-scatter.6
  655.0 28.5 reduce-scatter.8
  686.7 22.2 reduce-scatter.12
  712.6 150.6 all-reduce.10
where the time goes:
time: 888 us; the launch traced here: 876 us
  waiting for transfers between devices  237 us (27%)
  starting transfers between devices  201 us (23%)
  local copies, waits for them, and re-layouts  166 us (19%)
  other arithmetic  116 us (13%)
  blocking collectives  96.5 us (11%)
  matrix products  42.6 us (5%)
  between operations  14.6 us (2%)
    ppermute x2, starting transfers between devices, partner(): lax.ppermute(shard, axis, [(i, i ^ 1 << distance) for i in range(lax.axis...  144 us
    psum x1, waiting for transfers between devices, body(): lax.psum(merge_part_sum.astype(jnp.bfloat16), 'band').astype(jnp.float32)  77.6 us
    psum x1, blocking collectives, body(): lax.psum(gain_part_sum.astype(jnp.bfloat16), 'band').astype(jnp.float32)  75.3 us
    ppermute x9, starting transfers between devices, padded(): before = lax.ppermute(last, axis, up)  45.6 us
    slice x20, local copies, waits for them, and re-layouts, attend(): key_pairs = jnp.concatenate([kv_blocks[:-1], kv_blocks[1:]], axis=1)  38.4 us
    all_gather x1, waiting for transfers between devices, body(): lax.all_gather(qkv_weight, 'dp', axis=1, tiled=True)  32.2 us
    reduce_scatter x1, waiting for transfers between devices, body(): lax.psum_scatter(grad_sums[1][None].astype(jnp.bfloat16), 'dp', scatter_d...  31.1 us
    dynamic_update_slice x26, other arithmetic, place_one(): lax.dynamic_update_index_in_dim(buffer, jnp.where(active, new_value, curr...  30.9 us
  transfers between devices with their start and end apart: 27, of which 12 were waited for; matrix products, arithmetic and copies ran while one was open for 8% of the time, Pallas kernels for 0%

commit v1 on v0

--- a/solution.py
+++ b/solution.py
@@ -1,3 +1,4 @@
+import functools
 from functools import partial
 import jax
 import jax.numpy as jnp
@@ -11,6 +12,36 @@
 SW = 8
 EPSILON = 1e-05
 MASKED = -1e30
+
+
+def cover_table_now(inp, row_axis):
+    ready = lax.axis_size(row_axis)
+    met_up = lax.axis_index(row_axis)
+    local_next, a_next, upper = (ready, met_up, inp.shape[1])
+    row_list = [h * local_next if p == 1 else h for p, h in enumerate(inp.shape)]
+    mixed_arr = jnp.zeros(row_list, inp.dtype)
+    shaped = lax.dynamic_update_slice_in_dim(mixed_arr, inp, a_next * upper, axis=1)
+    right_arr = state_next = inp
+    for to_i in range(1, local_next // 2 + 1):
+        carry_out = range(local_next)
+        reply = map(lambda p: (p, (p + 1) % local_next), carry_out)
+        y = list(reply)
+        right_arr = lax.ppermute(right_arr, row_axis, y)
+        shaped = lax.dynamic_update_slice_in_dim(
+            shaped, right_arr, (a_next - to_i) % local_next * upper, axis=1
+        )
+        if 2 * to_i < local_next:
+            formed = range(local_next)
+            newest = map(lambda p: (p, (p - 1) % local_next), formed)
+            mat_out = list(newest)
+            state_next = lax.ppermute(state_next, row_axis, mat_out)
+            shaped = lax.dynamic_update_slice_in_dim(
+                shaped, state_next, (a_next + to_i) % local_next * upper, axis=1
+            )
+    return shaped
+
+
+manage_corner = functools.partial(cover_table_now, row_axis="dp")
 
 
 def padded(shard, sides, width):
@@ -186,7 +217,7 @@
 def body(fields, cell_mask, merge_weight, qkv_weight, out_weight, norm_gain, out_cotangent):
     merge_rows, qkv_rows, out_rows, gain_rows = (
         lax.all_gather(merge_weight, "dp", axis=1, tiled=True),
-        lax.all_gather(qkv_weight, "dp", axis=1, tiled=True),
+        manage_corner(qkv_weight),
         lax.all_gather(out_weight, "dp", axis=1, tiled=True),
         lax.all_gather(norm_gain, "dp", axis=1, tiled=True),
     )

time: 888 us -> 878 us (0.989)
  waiting for transfers between devices: 237 us -> 214 us
  starting transfers between devices: 201 us -> 216 us
    all_gather x1 -> x0, waiting for transfers between devices: 32.2 us -> none  [body(): lax.all_gather(qkv_weight, 'dp', axis=1, tiled=True)]
    ppermute x2, starting transfers between devices: 144 us -> 155 us  [partner(): lax.ppermute(shard, axis, [(i, i ^ 1 << distance) for i in range(lax.axis...]
    unnamed x8 -> x7, waiting for transfers between devices: 26.8 us -> 25.5 us
  transfers between devices with their start and end apart: 27 -> 29, of which waited for: 12 -> 11; matrix products, arithmetic and copies ran while one was open for 8% -> 8% of each run, Pallas kernels for 0% -> 0%
where the time goes in v1:
time: 878 us; the launch traced here: 867 us
  starting transfers between devices  216 us (25%)
  waiting for transfers between devices  214 us (24%)
  local copies, waits for them, and re-layouts  166 us (19%)
  other arithmetic  113 us (13%)
  blocking collectives  98.4 us (11%)
  matrix products  42.6 us (5%)
  between operations  14.8 us (2%)
    ppermute x2, starting transfers between devices, partner(): lax.ppermute(shard, axis, [(i, i ^ 1 << distance) for i in range(lax.axis...  155 us
    psum x1, waiting for transfers between devices, body(): lax.psum(merge_part_sum.astype(jnp.bfloat16), 'band').astype(jnp.float32)  77.5 us
    psum x1, blocking collectives, body(): lax.psum(gain_part_sum.astype(jnp.bfloat16), 'band').astype(jnp.float32)  75.2 us
    ppermute x9, starting transfers between devices, padded(): before = lax.ppermute(last, axis, up)  45.8 us
    slice x20, local copies, waits for them, and re-layouts, attend(): key_pairs = jnp.concatenate([kv_blocks[:-1], kv_blocks[1:]], axis=1)  38.3 us
    reduce_scatter x1, waiting for transfers between devices, body(): lax.psum_scatter(grad_sums[2][None].astype(jnp.bfloat16), 'dp', scatter_d...  32.4 us
    reduce_scatter x1, waiting for transfers between devices, body(): lax.psum_scatter(grad_sums[1][None].astype(jnp.bfloat16), 'dp', scatter_d...  31.1 us
    dynamic_update_slice x26, other arithmetic, place_one(): lax.dynamic_update_index_in_dim(buffer, jnp.where(active, new_value, curr...  30.9 us
  transfers between devices with their start and end apart: 29, of which 11 were waited for; matrix products, arithmetic and copies ran while one was open for 8% of the time, Pallas kernels for 0%

profile of v1, /device:TPU:2, one launch (start us, length us, event | category | flops | bytes accessed | tf_op | source)
XLA Modules:
  0.0 867.3 jit_solution(7019949298210601107)
XLA Ops:
  10.5 3.2 collective-permute-start.11
  15.2 14.8 %all_gather.11 = bf16[1,512,512]{2,1,0:T(8,128)(2,1)S(1)} all-gather(bf16[1,128,512]{2,1,0:T(8,128)(2,1)S(1)} %copy-done.44), channel_id=1, replica_groups=mesh['dp'=4,'segment'=2,'band'=32] {'dp'}, dimensions={1}, use_global_device_ids=true | all-gather | bytes 655360 | tf_op jit(solution)/shard_map/all_gather | solution.py:221
  30.0 8.4 all_gather.10
  39.2 7.8 collective-permute-done.10
  52.8 116.4 %while.103 = (s32[]{:T(128)}, bf16[2,8,16,512]{3,2,1,0:T(8,128)(2,1)}, bf16[2,8,16,1024]{3,2,1,0:T(8,128)(2,1)}, f32[2,8,16,512]{3,2,1,0:T(8,128)}, f32[2,8,16,1...) while((s32[]{:T(128)}, ...), condition=%wide.region_9.10_spmd, body=%wide.region_0.9_spmd.sunk | while | flops 477448448 | bytes 26721116 | solution.py:330
  53.8 5.3 conditional.18
  61.1 5.2 collective-permute-start.1
  79.6 27.4 %conditional.19 = (bf16[8,16,512]{2,1,0:T(8,128)(2,1)}, bf16[8,16,512]{2,1,0:T(8,128)(2,1)}) conditional(s32[]{:T(128)} %convert_element_type.561, () %tuple.323, (bf16[16,16,1024]{2,1,0:T(8,128)(2,1)}, pred[2,16,16]{2,1,0:T(8,128)(4,1)S(1)}, s32[]{:T(128)}, bf16[8,16,512]{2,1,0:T(8,128)(2,1)S(1)}, bf16[512,512]{1,0:T(8,128)(2,1)S(1)}, ...), branch_computations={%region_5.5_spmd, %region_6.8_spmd} | conditional | flops 137315840 | bytes 8476452 | solution.py:116
  97.6 3.2 fusion.210
  111.9 5.3 conditional.18
  119.3 5.2 collective-permute-start.1
  137.8 27.4 %conditional.19 = (bf16[8,16,512]{2,1,0:T(8,128)(2,1)}, bf16[8,16,512]{2,1,0:T(8,128)(2,1)}) conditional(s32[]{:T(128)} %convert_element_type.561, () %tuple.323, (bf16[16,16,1024]{2,1,0:T(8,128)(2,1)}, pred[2,16,16]{2,1,0:T(8,128)(4,1)S(1)}, s32[]{:T(128)}, bf16[8,16,512]{2,1,0:T(8,128)(2,1)S(1)}, bf16[512,512]{1,0:T(8,128)(2,1)S(1)}, ...), branch_computations={%region_5.5_spmd, %region_6.8_spmd} | conditional | flops 137315840 | bytes 8476452 | solution.py:116
  155.8 3.2 fusion.210
  169.2 12.2 %collective-permute-start.13 = (bf16[2,8,16,512]{3,2,1,0:T(8,128)(2,1)}, bf16[2,8,16,512]{3,2,1,0:T(8,128)(2,1)}, u32[]{:S(2)}, u32[]{:S(2)}) collective-permute-start(bf16[2,8,16,512]{3,2,1,0:T(8,128)(2,1)} %get-tuple-element.3200), channel_id=1, source_target_pairs={{0,32},{32,0},{1,33},{33,1},{2,34},{34,2},{3,35},{35,3},{4,36},{36... | collective-permute-start | bytes 786440 | tf_op jit(solution)/shard_map/ppermute | solution.py:61
  183.3 54.9 %while.104 = (s32[]{:T(128)}, bf16[2,8,16,512]{3,2,1,0:T(8,128)(2,1)}, bf16[2,8,16,1024]{3,2,1,0:T(8,128)(2,1)}, f32[2,8,16,512]{3,2,1,0:T(8,128)}, f32[2,8,16,1...) while((s32[]{:T(128)}, ...), condition=%wide.region_19.20_spmd, body=%wide.region_10.19_spmd.sunk | while | flops 477448448 | bytes 26721116 | solution.py:334
  187.8 5.2 collective-permute-start.3
  215.2 5.2 collective-permute-start.3
  238.9 60.7 %while.106 = (s32[]{:T(128)}, bf16[2,8,16,512]{3,2,1,0:T(8,128)(2,1)}, f32[1024,512]{1,0:T(8,128)}, f32[512,1536]{1,0:T(8,128)}, f32[512,512]{1,0:T(8,128)}, /*i...) while((s32[]{:T(128)}, ...), condition=%wide.region_33.34_spmd.clone, body=%wide.region_20.33_spmd.clone.sunk | while | flops 992495872 | bytes 121524072 | solution.py:343
  243.5 4.8 collective-permute-start.6
  261.7 3.7 select_add_fusion.8
  273.1 6.7 collective-permute-start.6
  281.1 2.7 select_add_fusion.10
  292.1 4.3 select_add_fusion.8
  299.6 143.2 %collective-permute-start.14 = (bf16[2,8,16,512]{3,2,1,0:T(8,128)(2,1)}, bf16[2,8,16,512]{3,2,1,0:T(8,128)(2,1)S(1)}, u32[]{:S(2)}, u32[]{:S(2)}) collective-permute-start(bf16[2,8,16,512]{3,2,1,0:T(8,128)(2,1)} %get-tuple-element.2101), channel_id=1, source_target_pairs={{0,32},{32,0},{1,33},{33,1},{2,34},{34,2},{3,35},{35,3},{4,36},{36... | collective-permute-start | bytes 786440 | tf_op jit(solution)/shard_map/ppermute | solution.py:61
  444.2 131.4 %while.105 = (s32[]{:T(128)}, f32[1024,512]{1,0:T(8,128)}, f32[512,1536]{1,0:T(8,128)}, f32[512,512]{1,0:T(8,128)}, f32[512]{0:T(512)}, /*index=5*/s32[]{:T(128)...) while((s32[]{:T(128)}, f32[1024,512]{1,0:T(8,128)}, ...), condition=%wide.region_47.48_spmd, body=%wide.region_34.47_spmd.sunk | while | flops 856311552 | bytes 123788608 | solution.py:350
  445.0 34.9 %conditional.22 = (bf16[8,16,512]{2,1,0:T(8,128)(2,1)}, bf16[16,16,1024]{2,1,0:T(8,128)(2,1)}, f32[512,512]{1,0:T(8,128)}) conditional(s32[]{:T(128)} %convert_element_type.565, () %tuple.339, (pred[2,16,16]{2,1,0:T(8,128)(4,1)S(1)}, s32[]{:T(128)}, bf16[8,16,512]{2,1,0:T(8,128)(2,1)}, bf16[512,512]{1,0:T(8,128)(2,1)S(1)}, ...), branch_computations={%region_35.35_spmd, %region_36.41_spmd} | conditional | flops 316294400 | bytes 26212748 | solution.py:116
  474.6 2.7 copy.87
  477.3 2.6 reshape.1713
  480.9 6.2 collective-permute-start.4
  491.3 2.8 collective-permute-done.5
  495.2 6.1 conditional.23
  497.9 2.8 convolution_bitcast_fusion.3
  503.0 4.3 add.982
  511.2 34.9 %conditional.22 = (bf16[8,16,512]{2,1,0:T(8,128)(2,1)}, bf16[16,16,1024]{2,1,0:T(8,128)(2,1)}, f32[512,512]{1,0:T(8,128)}) conditional(s32[]{:T(128)} %convert_element_type.565, () %tuple.339, (pred[2,16,16]{2,1,0:T(8,128)(4,1)S(1)}, s32[]{:T(128)}, bf16[8,16,512]{2,1,0:T(8,128)(2,1)}, bf16[512,512]{1,0:T(8,128)(2,1)S(1)}, ...), branch_computations={%region_35.35_spmd, %region_36.41_spmd} | conditional | flops 316294400 | bytes 26212748 | solution.py:116
  540.8 2.7 copy.87
  543.5 2.6 reshape.1713
  547.1 4.1 collective-permute-start.4
  555.3 4.0 collective-permute-done.5
  560.4 6.1 conditional.23
  563.1 2.8 convolution_bitcast_fusion.3
  568.2 4.3 add.982
  577.8 2.9 convert_bitcast_fusion.1
  583.1 32.4 %reduce-scatter.11.cloned.1.call-done = bf16[1,128,512]{2,1,0:T(8,128)(2,1)} async-done(((bf16[1,512,512]{2,1,0:T(8,128)(2,1)}), bf16[1,128,512]{2,1,0:T(8,128)(2,1)}) %reduce-scatter.11.cloned.1.call-update) | async-done | bytes 131088 | tf_op jit(solution)/shard_map/reduce_scatter | solution.py:361
  615.5 28.5 %reduce-scatter.7.cloned.1.call-done = bf16[1,256,512]{2,1,0:T(8,128)(2,1)} async-done(((bf16[1,1024,512]{2,1,0:T(8,128)(2,1)}), bf16[1,256,512]{2,1,0:T(8,128)(2,1)}) %reduce-scatter.7.cloned.1.call-update) | async-done | bytes 262160 | tf_op jit(solution)/shard_map/reduce_scatter | solution.py:355
  644.1 31.1 %reduce-scatter.9.cloned.1.call-done = bf16[1,128,1536]{2,1,0:T(8,128)(2,1)} async-done(((bf16[1,512,1536]{2,1,0:T(8,128)(2,1)}), bf16[1,128,1536]{2,1,0:T(8,128)(2,1)}) %reduce-scatter.9.cloned.1.call-update) | async-done | bytes 393232 | tf_op jit(solution)/shard_map/reduce_scatter | solution.py:358
  675.2 25.4 %reduce-scatter.13.cloned.1.call-done = bf16[128,1]{1,0:T(8,128)(2,1)} async-done(((bf16[512,1]{1,0:T(8,128)(2,1)}), bf16[128,1]{1,0:T(8,128)(2,1)}) %reduce-scatter.13.cloned.1.call-update) | async-done | bytes 272
  701.4 75.2 %psum.31 = bf16[1,128]{1,0:T(2,128)(2,1)S(1)} all-reduce(bf16[1,128]{1,0:T(2,128)(2,1)S(1)} %copy.91), channel_id=1, replica_groups=mesh['dp'=4,'segment'=2,'band'=32] {'band'}, use_global_device_ids=true, to_apply=%region_55.56 | all-reduce | flops 128 | bytes 512 | tf_op jit(solution)/shard_map/psum | solution.py:372
  777.1 77.5 %all-reduce.11.cloned.1.call-done = (bf16[1,256,512]{2,1,0:T(8,128)(2,1)}, bf16[1,128,1536]{2,1,0:T(8,128)(2,1)}, bf16[1,128,512]{2,1,0:T(8,128)(2,1)}) async-done(((bf16[1,256,512]{2,1,0:T(8,128)(2,1)}, bf16[1,128,1536]{2,1,0:T(8,128)(2,1)}, bf16[1,128,512]{2,1,0:T(8,128)(2,1)}), (bf16[1,256,512]{2,1,0:T(8,128)(2,1)}, bf16[1,128,1536]{2,1,0:T(8,128)(2,1)}, ...) | async-done | bytes 786448 | tf_op jit(solution)/shard_map/psum | solution.py:369
  (498 shorter events, 310.7 us)
Async XLA Ops:
  7.2 7.9 copy-start.39
  7.2 31.2 %copy-start.45 = (s32[1,2,8,16]{3,2,1,0:T(8,128)S(1)}, s32[1,2,8,16]{3,2,1,0:T(8,128)}, u32[]{:S(2)}) copy-start(s32[1,2,8,16]{3,2,1,0:T(8,128)} %param.32) | copy-start | bytes 3076
  7.2 8.0 copy-start.44
  7.2 22.8 %copy-start.46 = (bf16[1,128]{1,0:T(2,128)(2,1)S(1)}, bf16[1,128]{1,0:T(2,128)(2,1)}, u32[]{:S(2)}) copy-start(bf16[1,128]{1,0:T(2,128)(2,1)} %param.36) | copy-start | bytes 772
  7.2 39.8 %all-gather.2.cloned.1.call-start = ((), (), s32[]{:S(2)}) async-start(), calls=%async_computation.4 | async-start | bytes 1310720 | tf_op jit(solution)/shard_map/all_gather | solution.py:219
  7.3 31.9 %collective-permute-start.9 = (bf16[1,128,1536]{2,1,0:T(8,128)(2,1)}, bf16[1,128,1536]{2,1,0:T(8,128)(2,1)S(1)}, u32[]{:S(2)}, u32[]{:S(2)}) collective-permute-start(bf16[1,128,1536]{2,1,0:T(8,128)(2,1)} %param.34), channel_id=1, source_target_pairs={{0,192},{64,0},{128,64},{192,128},{1,193},{65,1},{129,65},{193,129... | collective-permute-start | bytes 1179656 | tf_op jit(solution)/shard_map/ppermute | solution.py:37
  9.6 28.8 %collective-permute-start.8 = (bf16[1,128,1536]{2,1,0:T(8,128)(2,1)}, bf16[1,128,1536]{2,1,0:T(8,128)(2,1)S(1)}, u32[]{:S(2)}, u32[]{:S(2)}) collective-permute-start(bf16[1,128,1536]{2,1,0:T(8,128)(2,1)} %param.34), channel_id=1, source_target_pairs={{0,64},{64,128},{128,192},{192,0},{1,65},{65,129},{129,193},{193,1... | collective-permute-start | bytes 1179656 | tf_op jit(solution)/shard_map/ppermute | solution.py:29
  9.6 605.9 %reduce-scatter.11.cloned.1.call-start = ((), (), s32[]{:S(2)}) async-start(), calls=%async_computation.7 | async-start | bytes 655360 | tf_op jit(solution)/shard_map/reduce_scatter | solution.py:361
  10.5 27.9 %collective-permute-start.11 = (s32[2,4,16]{2,1,0:T(4,128)S(1)}, s32[2,4,16]{2,1,0:T(4,128)S(1)}, u32[]{:S(2)}, u32[]{:S(2)}) collective-permute-start(s32[2,4,16]{2,1,0:T(4,128)S(1)} %get-tuple-element.2527), channel_id=1, source_target_pairs={{0,1},{1,2},{2,3},{3,4},{4,5},{5,6},{6,7},{7,8},{8,9},{9,10},{10,1... | collective-permute-start | bytes 1544 | tf_op jit(solution)/shard_map/ppermute | solution.py:54
  13.7 24.7 %collective-permute-start.12 = (s32[2,4,16]{2,1,0:T(4,128)S(1)}, s32[2,4,16]{2,1,0:T(4,128)S(1)}, u32[]{:S(2)}, u32[]{:S(2)}) collective-permute-start(s32[2,4,16]{2,1,0:T(4,128)S(1)} %get-tuple-element.2528), channel_id=1, source_target_pairs={{1,0},{2,1},{3,2},{4,3},{5,4},{6,5},{7,6},{8,7},{9,8},{10,9},{11,1... | collective-permute-start | bytes 1544 | tf_op jit(solution)/shard_map/ppermute | solution.py:55
  38.4 8.5 collective-permute-start.10
  59.0 14.0 %copy-start.25 = (bf16[2,8,16,512]{3,2,1,0:T(8,128)(2,1)S(1)}, bf16[2,8,16,512]{3,2,1,0:T(8,128)(2,1)}, u32[]{:S(2)}) copy-start(bf16[2,8,16,512]{3,2,1,0:T(8,128)(2,1)} %get-tuple-element.3164) | copy-start | bytes 786436 | tf_op jit(solution)/shard_map/while
  59.0 16.3 %copy-start.31 = (bf16[2,8,16,512]{3,2,1,0:T(8,128)(2,1)S(1)}, bf16[2,8,16,512]{3,2,1,0:T(8,128)(2,1)}, u32[]{:S(2)}) copy-start(bf16[2,8,16,512]{3,2,1,0:T(8,128)(2,1)} %get-tuple-element.3160) | copy-start | bytes 786436 | tf_op jit(solution)/shard_map/while
  59.8 18.0 %collective-permute-start = (bf16[4,16,1024]{2,1,0:T(8,128)(2,1)}, bf16[4,16,1024]{2,1,0:T(8,128)(2,1)}, u32[]{:S(2)}, u32[]{:S(2)}) collective-permute-start(bf16[4,16,1024]{2,1,0:T(8,128)(2,1)} %get-tuple-element.2975), channel_id=1, source_target_pairs={{1,0},{2,1},{3,2},{4,3},{5,4},{6,5},{7,6},{8,7},{9,8},{10,9},{11,1... | collective-permute-start | bytes 393224 | tf_op jit(solution)/shard_map/while/body/eval_jaxpr/ppermute | solution.py:55
  61.1 16.7 %collective-permute-start.1 = (bf16[4,16,1024]{2,1,0:T(8,128)(2,1)}, bf16[4,16,1024]{2,1,0:T(8,128)(2,1)}, u32[]{:S(2)}, u32[]{:S(2)}) collective-permute-start(bf16[4,16,1024]{2,1,0:T(8,128)(2,1)} %get-tuple-element.2976), channel_id=1, source_target_pairs={{0,1},{1,2},{2,3},{3,4},{4,5},{5,6},{6,7},{7,8},{8,9},{9,10},{10,1... | collective-permute-start | bytes 393224 | tf_op jit(solution)/shard_map/while/body/eval_jaxpr/ppermute | solution.py:54
  117.2 14.0 %copy-start.25 = (bf16[2,8,16,512]{3,2,1,0:T(8,128)(2,1)S(1)}, bf16[2,8,16,512]{3,2,1,0:T(8,128)(2,1)}, u32[]{:S(2)}) copy-start(bf16[2,8,16,512]{3,2,1,0:T(8,128)(2,1)} %get-tuple-element.3164) | copy-start | bytes 786436 | tf_op jit(solution)/shard_map/while
  117.2 16.3 %copy-start.31 = (bf16[2,8,16,512]{3,2,1,0:T(8,128)(2,1)S(1)}, bf16[2,8,16,512]{3,2,1,0:T(8,128)(2,1)}, u32[]{:S(2)}) copy-start(bf16[2,8,16,512]{3,2,1,0:T(8,128)(2,1)} %get-tuple-element.3160) | copy-start | bytes 786436 | tf_op jit(solution)/shard_map/while
  118.0 18.0 %collective-permute-start = (bf16[4,16,1024]{2,1,0:T(8,128)(2,1)}, bf16[4,16,1024]{2,1,0:T(8,128)(2,1)}, u32[]{:S(2)}, u32[]{:S(2)}) collective-permute-start(bf16[4,16,1024]{2,1,0:T(8,128)(2,1)} %get-tuple-element.2975), channel_id=1, source_target_pairs={{1,0},{2,1},{3,2},{4,3},{5,4},{6,5},{7,6},{8,7},{9,8},{10,9},{11,1... | collective-permute-start | bytes 393224 | tf_op jit(solution)/shard_map/while/body/eval_jaxpr/ppermute | solution.py:55
  119.3 16.7 %collective-permute-start.1 = (bf16[4,16,1024]{2,1,0:T(8,128)(2,1)}, bf16[4,16,1024]{2,1,0:T(8,128)(2,1)}, u32[]{:S(2)}, u32[]{:S(2)}) collective-permute-start(bf16[4,16,1024]{2,1,0:T(8,128)(2,1)} %get-tuple-element.2976), channel_id=1, source_target_pairs={{0,1},{1,2},{2,3},{3,4},{4,5},{5,6},{6,7},{7,8},{8,9},{9,10},{10,1... | collective-permute-start | bytes 393224 | tf_op jit(solution)/shard_map/while/body/eval_jaxpr/ppermute | solution.py:54
  169.2 14.1 %collective-permute-start.13 = (bf16[2,8,16,512]{3,2,1,0:T(8,128)(2,1)}, bf16[2,8,16,512]{3,2,1,0:T(8,128)(2,1)}, u32[]{:S(2)}, u32[]{:S(2)}) collective-permute-start(bf16[2,8,16,512]{3,2,1,0:T(8,128)(2,1)} %get-tuple-element.3200), channel_id=1, source_target_pairs={{0,32},{32,0},{1,33},{33,1},{2,34},{34,2},{3,35},{35,3},{4,36},{36... | collective-permute-start | bytes 786440 | tf_op jit(solution)/shard_map/ppermute | solution.py:61
  185.8 14.0 %copy-start.27 = (bf16[2,8,16,512]{3,2,1,0:T(8,128)(2,1)S(1)}, bf16[2,8,16,512]{3,2,1,0:T(8,128)(2,1)}, u32[]{:S(2)}) copy-start(bf16[2,8,16,512]{3,2,1,0:T(8,128)(2,1)} %get-tuple-element.3224) | copy-start | bytes 786436 | tf_op jit(solution)/shard_map/while
  185.8 15.4 %copy-start.32 = (bf16[2,8,16,512]{3,2,1,0:T(8,128)(2,1)S(1)}, bf16[2,8,16,512]{3,2,1,0:T(8,128)(2,1)}, u32[]{:S(2)}) copy-start(bf16[2,8,16,512]{3,2,1,0:T(8,128)(2,1)} %get-tuple-element.3220) | copy-start | bytes 786436 | tf_op jit(solution)/shard_map/while
  186.5 17.1 %collective-permute-start.2 = (bf16[4,16,1024]{2,1,0:T(8,128)(2,1)}, bf16[4,16,1024]{2,1,0:T(8,128)(2,1)}, u32[]{:S(2)}, u32[]{:S(2)}) collective-permute-start(bf16[4,16,1024]{2,1,0:T(8,128)(2,1)} %get-tuple-element.3006), channel_id=1, source_target_pairs={{1,0},{2,1},{3,2},{4,3},{5,4},{6,5},{7,6},{8,7},{9,8},{10,9},{11,1... | collective-permute-start | bytes 393224 | tf_op jit(solution)/shard_map/while/body/eval_jaxpr/ppermute | solution.py:55
  187.8 15.9 %collective-permute-start.3 = (bf16[4,16,1024]{2,1,0:T(8,128)(2,1)}, bf16[4,16,1024]{2,1,0:T(8,128)(2,1)}, u32[]{:S(2)}, u32[]{:S(2)}) collective-permute-start(bf16[4,16,1024]{2,1,0:T(8,128)(2,1)} %get-tuple-element.3007), channel_id=1, source_target_pairs={{0,1},{1,2},{2,3},{3,4},{4,5},{5,6},{6,7},{7,8},{8,9},{9,10},{10,1... | collective-permute-start | bytes 393224 | tf_op jit(solution)/shard_map/while/body/eval_jaxpr/ppermute | solution.py:54
  213.2 14.0 %copy-start.27 = (bf16[2,8,16,512]{3,2,1,0:T(8,128)(2,1)S(1)}, bf16[2,8,16,512]{3,2,1,0:T(8,128)(2,1)}, u32[]{:S(2)}) copy-start(bf16[2,8,16,512]{3,2,1,0:T(8,128)(2,1)} %get-tuple-element.3224) | copy-start | bytes 786436 | tf_op jit(solution)/shard_map/while
  213.2 15.4 %copy-start.32 = (bf16[2,8,16,512]{3,2,1,0:T(8,128)(2,1)S(1)}, bf16[2,8,16,512]{3,2,1,0:T(8,128)(2,1)}, u32[]{:S(2)}) copy-start(bf16[2,8,16,512]{3,2,1,0:T(8,128)(2,1)} %get-tuple-element.3220) | copy-start | bytes 786436 | tf_op jit(solution)/shard_map/while
  213.9 17.1 %collective-permute-start.2 = (bf16[4,16,1024]{2,1,0:T(8,128)(2,1)}, bf16[4,16,1024]{2,1,0:T(8,128)(2,1)}, u32[]{:S(2)}, u32[]{:S(2)}) collective-permute-start(bf16[4,16,1024]{2,1,0:T(8,128)(2,1)} %get-tuple-element.3006), channel_id=1, source_target_pairs={{1,0},{2,1},{3,2},{4,3},{5,4},{6,5},{7,6},{8,7},{9,8},{10,9},{11,1... | collective-permute-start | bytes 393224 | tf_op jit(solution)/shard_map/while/body/eval_jaxpr/ppermute | solution.py:55
  215.2 15.9 %collective-permute-start.3 = (bf16[4,16,1024]{2,1,0:T(8,128)(2,1)}, bf16[4,16,1024]{2,1,0:T(8,128)(2,1)}, u32[]{:S(2)}, u32[]{:S(2)}) collective-permute-start(bf16[4,16,1024]{2,1,0:T(8,128)(2,1)} %get-tuple-element.3007), channel_id=1, source_target_pairs={{0,1},{1,2},{2,3},{3,4},{4,5},{5,6},{6,7},{7,8},{8,9},{9,10},{10,1... | collective-permute-start | bytes 393224 | tf_op jit(solution)/shard_map/while/body/eval_jaxpr/ppermute | solution.py:54
  241.8 12.0 %copy-start.21 = (bf16[8,16,512]{2,1,0:T(8,128)(2,1)}, bf16[8,16,512]{2,1,0:T(8,128)(2,1)S(1)}, u32[]{:S(2)}) copy-start(bf16[8,16,512]{2,1,0:T(8,128)(2,1)S(1)} %get-tuple-element.3070) | copy-start | bytes 393220 | tf_op jit(solution)/shard_map/while
  243.5 11.9 %collective-permute-start.6 = (bf16[4,16,1024]{2,1,0:T(8,128)(2,1)}, bf16[4,16,1024]{2,1,0:T(8,128)(2,1)}, u32[]{:S(2)}, u32[]{:S(2)}) collective-permute-start(bf16[4,16,1024]{2,1,0:T(8,128)(2,1)} %get-tuple-element.3072), channel_id=1, source_target_pairs={{0,1},{1,2},{2,3},{3,4},{4,5},{5,6},{6,7},{7,8},{8,9},{9,10},{10,1... | collective-permute-start | bytes 393224 | tf_op jit(solution)/shard_map/while/body/eval_jaxpr/ppermute | solution.py:54
  248.3 8.4 collective-permute-start.7
  271.4 14.2 %copy-start.21 = (bf16[8,16,512]{2,1,0:T(8,128)(2,1)}, bf16[8,16,512]{2,1,0:T(8,128)(2,1)S(1)}, u32[]{:S(2)}) copy-start(bf16[8,16,512]{2,1,0:T(8,128)(2,1)S(1)} %get-tuple-element.3070) | copy-start | bytes 393220 | tf_op jit(solution)/shard_map/while
  273.1 14.1 %collective-permute-start.6 = (bf16[4,16,1024]{2,1,0:T(8,128)(2,1)}, bf16[4,16,1024]{2,1,0:T(8,128)(2,1)}, u32[]{:S(2)}, u32[]{:S(2)}) collective-permute-start(bf16[4,16,1024]{2,1,0:T(8,128)(2,1)} %get-tuple-element.3072), channel_id=1, source_target_pairs={{0,1},{1,2},{2,3},{3,4},{4,5},{5,6},{6,7},{7,8},{8,9},{9,10},{10,1... | collective-permute-start | bytes 393224 | tf_op jit(solution)/shard_map/while/body/eval_jaxpr/ppermute | solution.py:54
  279.8 7.4 collective-permute-start.7
  299.6 144.6 %collective-permute-start.14 = (bf16[2,8,16,512]{3,2,1,0:T(8,128)(2,1)}, bf16[2,8,16,512]{3,2,1,0:T(8,128)(2,1)S(1)}, u32[]{:S(2)}, u32[]{:S(2)}) collective-permute-start(bf16[2,8,16,512]{3,2,1,0:T(8,128)(2,1)} %get-tuple-element.2101), channel_id=1, source_target_pairs={{0,32},{32,0},{1,33},{33,1},{2,34},{34,2},{3,35},{35,3},{4,36},{36... | collective-permute-start | bytes 786440 | tf_op jit(solution)/shard_map/ppermute | solution.py:61
  445.0 43.4 %copy-start.10 = (f32[512,512]{1,0:T(8,128)S(1)}, f32[512,512]{1,0:T(8,128)}, u32[]{:S(2)}) copy-start(f32[512,512]{1,0:T(8,128)} %get-tuple-element.3359) | copy-start | bytes 3145732 | tf_op jit(solution)/shard_map/while
  480.9 10.3 %collective-permute-start.4 = (bf16[4,16,1024]{2,1,0:T(8,128)(2,1)S(1)}, bf16[4,16,1024]{2,1,0:T(8,128)(2,1)}, u32[]{:S(2)}, u32[]{:S(2)}) collective-permute-start(bf16[4,16,1024]{2,1,0:T(8,128)(2,1)S(1)} %get-tuple-element.3040), channel_id=1, source_target_pairs={{0,1},{1,2},{2,3},{3,4},{4,5},{5,6},{6,7},{7,8},{8,9},{9,10},{10,1... | collective-permute-start | bytes 393224 | tf_op jit(solution)/shard_map/while/body/eval_jaxpr/ppermute | solution.py:54
  487.1 7.0 collective-permute-start.5
  511.2 41.3 %copy-start.10 = (f32[512,512]{1,0:T(8,128)S(1)}, f32[512,512]{1,0:T(8,128)}, u32[]{:S(2)}) copy-start(f32[512,512]{1,0:T(8,128)} %get-tuple-element.3359) | copy-start | bytes 3145732 | tf_op jit(solution)/shard_map/while
  547.1 8.2 collective-permute-start.4
  551.2 8.1 collective-permute-start.5
  552.5 7.9 copy-start.17
  552.5 7.9 copy-start.22
  552.5 7.9 copy-start.30
  577.8 66.3 %reduce-scatter.7.cloned.1.call-start = ((), (), s32[]{:S(2)}) async-start(), calls=%async_computation.5 | async-start | bytes 1310720 | tf_op jit(solution)/shard_map/reduce_scatter | solution.py:355
  580.7 94.5 %reduce-scatter.9.cloned.1.call-start = ((), (), s32[]{:S(2)}) async-start(), calls=%async_computation.6 | async-start | bytes 1966080 | tf_op jit(solution)/shard_map/reduce_scatter | solution.py:358
  582.1 118.4 %reduce-scatter.13.cloned.1.call-start = ((), (), s32[]{:S(2)}) async-start(), calls=%async_computation.8 | async-start | bytes 163840
  583.0 271.6 %all-reduce.11.cloned.1.call-start = ((), (), s32[]{:S(2)}) async-start(), calls=%async_computation.9 | async-start | bytes 1572864 | tf_op jit(solution)/shard_map/psum | solution.py:369
  (54 other events, 141.5 us)
Sparse Core Ops, SparseCore 0:
  9.8 30.4 all-gather.1
  577.9 37.5 reduce-scatter.10
  618.1 25.9 reduce-scatter.6
  646.6 28.4 reduce-scatter.8
  678.2 22.2 reduce-scatter.12
  704.0 150.5 all-reduce.10
